TPU v7x, 32 devices: a whole 2x2x4 slice. The times are simulated.
32 devices in a mesh: groups: 2 (over x), fsdp: 8 (over z, y), head: 2 (over core).
Axes of the slice: x: 2, y: 2, z: 4, core: 2. Of those that a mesh axis runs over, the one named last changes fastest.
Arguments:
- activations: bfloat16 [4096, 16384], P(('groups', 'fsdp'), 'head'), parts along dimension 0, may hold values from -6 to 6
- queries: bfloat16 [4096, 8192], P(('groups', 'fsdp'), 'head'), parts along dimension 0, may hold values from -400 to 400
- w_key: bfloat16 [16384, 512], P('fsdp', 'head'), may hold values from -0.046875 to 0.046875
- w_value: bfloat16 [16384, 512], P('fsdp', 'head'), may hold values from -0.046875 to 0.046875
- request_pages: int32 [16], P('groups'), parts along dimension 0, may hold values from 1 to 7, 16 in all
- request_owner: int32 [16], P('groups'), parts along dimension 0, may hold values from 0 to 7, each once
Outputs:
- attended: bfloat16 [4096, 8192], P(('groups', 'fsdp'), 'head'), parts along dimension 0
- kv_cache: bfloat16 [112, 2, 128, 512], P(('groups', 'fsdp'), None, None, 'head'), parts along dimension 0
There are 2 independent parts, one for each index of `groups`. A program takes and returns all parts, laid end to end along the dimension named above; an argument that names none is the same for every part. Nothing has to cross between parts.
Inputs may be any that keep to these rules, and one draw needn't show every extreme that they name: `request_pages`: the requests' page counts sum to 16, and the longest has exactly 7 pages. `request_owner`: each decode device owns exactly one request.
All inputs are finite; a program needn't handle non-finite values.
Results may differ from a plain program's by a relative error of at most 0.012.
The roundings to bfloat16 on the way count: a program that leaves them out, or rounds other values in their place, can miss the bound.
Values may be sent and summed in bfloat16 or wider, within the bound.
A program may use at most 128 MiB of HBM per device.

v0:
```python
import jax
import jax.numpy as jnp
from jax import lax
from jax.sharding import PartitionSpec as P

QH = 64
KVH = 4
HD = 128
PAGE = 128
SPAN = 3


def shifted(array, axis, by):
    count = lax.axis_size(axis)
    pairs = [(i, i + by) for i in range(count) if 0 <= i + by < count]
    return lax.ppermute(array, axis, pairs)


def token_docs(first_tok, count, doc_ends):
    positions = first_tok + jnp.arange(count, dtype=jnp.int32)
    pages = positions // PAGE
    found = jnp.sum((doc_ends[None, :] <= pages[:, None]).astype(jnp.int32), axis=1)
    return (jnp.where(positions >= 0, found, -1), positions)


def page_slot(global_pages, doc_ends, doc_begins, request_owner, cache_pages):
    count = doc_ends.shape[0]
    found = jnp.sum((doc_ends[None, :] <= global_pages[:, None]).astype(jnp.int32), axis=1)
    matched = found[:, None] == jnp.arange(count, dtype=jnp.int32)[None, :]
    owner_dev = jnp.sum(jnp.where(matched, request_owner[None, :], 0), axis=1)
    doc_begin = jnp.sum(jnp.where(matched, doc_begins[None, :], 0), axis=1)
    return owner_dev * cache_pages + global_pages - doc_begin


def masked_scores(query_head, key_head, visible, score_scale):
    scores = (
        jnp.einsum("tqd,sd->qts", query_head, key_head, preferred_element_type=jnp.float32)
        * score_scale
    )
    return jnp.where(visible[None], scores, -1e30)


def per_device(activations, queries, w_key, w_value, request_pages, request_owner):
    tok_rows = activations.shape[0]
    width_kv = w_key.shape[1]
    kv_here = width_kv // HD
    per_group = QH // KVH
    n_dev = lax.axis_size("fsdp")
    my_index = lax.axis_index("fsdp")
    score_scale = HD ** (-0.5)
    full_rows = lax.all_gather(activations, "head", axis=1, tiled=True)
    key_sum = jnp.dot(
        full_rows,
        lax.all_gather(w_key, "fsdp", axis=0, tiled=True),
        preferred_element_type=jnp.float32,
    )
    value_sum = jnp.dot(
        full_rows,
        lax.all_gather(w_value, "fsdp", axis=0, tiled=True),
        preferred_element_type=jnp.float32,
    )
    key_rows = key_sum.astype(jnp.bfloat16)
    value_rows = value_sum.astype(jnp.bfloat16)
    doc_ends = jnp.cumsum(request_pages)
    doc_begins = doc_ends - request_pages
    first_tok = my_index * tok_rows
    query_docs, query_pos = token_docs(first_tok, tok_rows, doc_ends)
    blocks = [(key_rows, value_rows, first_tok)]
    for distance in range(1, SPAN + 1):
        near_k, near_v = shifted((key_rows, value_rows), "fsdp", distance)
        blocks.append((near_k, near_v, first_tok - distance * tok_rows))
    described = []
    for index, (block_k, block_v, block_first) in enumerate(blocks):
        key_docs, key_pos = token_docs(block_first, tok_rows, doc_ends)
        visible = (key_docs[None, :] == query_docs[:, None]) & (
            key_pos[None, :] <= query_pos[:, None]
        )
        live = None if index == 0 else key_docs[tok_rows - 1] == query_docs[0]
        described.append((block_k, block_v, visible, live))
    query_all = queries.reshape(tok_rows, kv_here, per_group, HD)
    head_outputs = []
    for kv_index in range(kv_here):
        query_head = query_all[:, kv_index]
        low = kv_index * HD
        key_head = jnp.concatenate([item[0][:, low : low + HD] for item in described], 0)
        value_head = jnp.concatenate([item[1][:, low : low + HD] for item in described], 0)
        visible = jnp.concatenate([item[2] for item in described], 1)
        scores = masked_scores(query_head, key_head, visible, score_scale)
        row_top = jnp.max(scores, axis=-1, keepdims=True)
        expo = jnp.where(visible[None], jnp.exp(scores - row_top), 0.0)
        row_total = jnp.sum(expo, axis=-1)
        weights = expo.astype(jnp.bfloat16)
        weighted = jnp.einsum(
            "qts,sd->tqd", weights, value_head, preferred_element_type=jnp.float32
        )
        head_outputs.append(weighted / jnp.transpose(row_total, (1, 0))[:, :, None])
    attended = (
        jnp.stack(head_outputs, axis=1)
        .reshape(tok_rows, kv_here * per_group * HD)
        .astype(jnp.bfloat16)
    )
    pages_here = tok_rows // PAGE
    cache_pages = SPAN * pages_here + 1
    page_data = jnp.stack(
        [
            key_rows.reshape(pages_here, PAGE, width_kv),
            value_rows.reshape(pages_here, PAGE, width_kv),
        ],
        axis=1,
    )
    flat_pages = page_data.reshape(pages_here, 2 * PAGE * width_kv)
    slot_ids = jnp.arange(cache_pages, dtype=jnp.int32)
    own_pages = my_index * pages_here + jnp.arange(pages_here, dtype=jnp.int32)
    target = page_slot(own_pages, doc_ends, doc_begins, request_owner, cache_pages) // cache_pages
    routed = target[None, :] == jnp.arange(n_dev, dtype=jnp.int32)[:, None]
    outgoing = jnp.where(routed[:, :, None], flat_pages[None], jnp.zeros((), jnp.bfloat16))
    incoming = lax.all_to_all(outgoing, "fsdp", split_axis=0, concat_axis=0, tiled=True)
    incoming = incoming.reshape(n_dev * pages_here, 2 * PAGE * width_kv)
    source_pages = jnp.arange(n_dev * pages_here, dtype=jnp.int32)
    local_slot = (
        page_slot(source_pages, doc_ends, doc_begins, request_owner, cache_pages)
        - my_index * cache_pages
    )
    selector = (local_slot[None, :] == slot_ids[:, None]).astype(jnp.bfloat16)
    cache_sum = jnp.dot(selector, incoming, preferred_element_type=jnp.float32)
    kv_cache = cache_sum.astype(jnp.bfloat16).reshape(cache_pages, 2, PAGE, width_kv)
    return (attended, kv_cache)


def solution(mesh):
    return jax.shard_map(
        per_device,
        mesh=mesh,
        in_specs=(
            P(("groups", "fsdp"), "head"),
            P(("groups", "fsdp"), "head"),
            P("fsdp", "head"),
            P("fsdp", "head"),
            P("groups"),
            P("groups"),
        ),
        out_specs=(P(("groups", "fsdp"), "head"), P(("groups", "fsdp"), None, None, "head")),
        check_vma=False,
    )
```

profile of v0, /device:TPU:14, one launch (start us, length us, event | category | flops | bytes accessed | tf_op | source)
XLA Modules:
  0.0 413.6 jit_solution(15465070905032131087)
XLA Ops:
  9.4 4.1 copy.23
  14.9 15.9 %all-gather.4.cloned.1.call-done = bf16[256,16384]{1,0:T(8,128)(2,1)} async-done(((bf16[256,8192]{1,0:T(8,128)(2,1)}), bf16[256,16384]{1,0:T(8,128)(2,1)}) %all-gather.4.cloned.1.call-update) | async-done | bytes 8388624 | tf_op jit(solution)/shard_map/all_gather | solution.py:51
  30.8 125.2 %all-gather.6.cloned.1.call-done = bf16[16384,256]{1,0:T(8,128)(2,1)} async-done(((bf16[2048,256]{1,0:T(8,128)(2,1)}), bf16[16384,256]{1,0:T(8,128)(2,1)}) %all-gather.6.cloned.1.call-update) | async-done | bytes 8388624 | tf_op jit(solution)/shard_map/all_gather | solution.py:59
  156.0 8.1 %convolution_convert_fusion.2 = bf16[256,256]{1,0:T(8,128)(2,1)S(1)} fusion(bf16[256,16384]{1,0:T(8,128)(2,1)} %all-gather.4.cloned.1.call-done, bf16[16384,256]{1,0:T(8,128)(2,1)} %all-gather.6.cloned.1.call-done), kind=kOutput, calls=%fused_computation.30 | convolution fusion | flops 2147549184 | bytes 16908288 | tf_op jit(solution)/shard_map/dot_general | solution.py:57
  164.1 5.1 %collective-permute-start.2 = (bf16[256,256]{1,0:T(8,128)(2,1)S(1)}, bf16[256,256]{1,0:T(8,128)(2,1)S(1)}, u32[]{:S(2)}, u32[]{:S(2)}) collective-permute-start(bf16[256,256]{1,0:T(8,128)(2,1)S(1)} %convolution_convert_fusion.2), channel_id=1, source_target_pairs={{0,6},{2,8},{4,10},{6,12},{8,14},{1,7},{3,9},{5,11},{7,13},{9,15},... | collective-permute-start | bytes 393224 | tf_op jit(solution)/shard_map/ppermute | solution.py:16
  169.3 1.9 collective-permute-start.1
  171.2 2.5 collective-permute-start
  173.7 118.6 %all-gather.8.cloned.1.call-done = bf16[16384,256]{1,0:T(8,128)(2,1)} async-done(((bf16[2048,256]{1,0:T(8,128)(2,1)}), bf16[16384,256]{1,0:T(8,128)(2,1)}) %all-gather.8.cloned.1.call-update) | async-done | bytes 8388624 | tf_op jit(solution)/shard_map/all_gather | solution.py:54
  292.3 8.1 %convolution_convert_fusion.1 = bf16[256,256]{1,0:T(8,128)(2,1)S(1)} fusion(bf16[256,16384]{1,0:T(8,128)(2,1)} %all-gather.4.cloned.1.call-done, bf16[16384,256]{1,0:T(8,128)(2,1)} %all-gather.8.cloned.1.call-done), kind=kOutput, calls=%fused_computation.29 | convolution fusion | flops 2147549184 | bytes 16908288 | tf_op jit(solution)/shard_map/dot_general | solution.py:52
  300.4 5.1 %collective-permute-start.5 = (bf16[256,256]{1,0:T(8,128)(2,1)S(1)}, bf16[256,256]{1,0:T(8,128)(2,1)S(1)}, u32[]{:S(2)}, u32[]{:S(2)}) collective-permute-start(bf16[256,256]{1,0:T(8,128)(2,1)S(1)} %convolution_convert_fusion.1), channel_id=1, source_target_pairs={{0,6},{2,8},{4,10},{6,12},{8,14},{1,7},{3,9},{5,11},{7,13},{9,15},... | collective-permute-start | bytes 393224 | tf_op jit(solution)/shard_map/ppermute | solution.py:16
  305.6 1.9 collective-permute-start.4
  307.8 3.2 broadcast_select_fusion
  311.1 5.6 %all-to-all-start = ((bf16[8,2,65536]{2,1,0:T(2,128)(2,1)}), bf16[8,2,65536]{2,1,0:T(2,128)(2,1)S(1)}, u32[]{:S(2)}, u32[]{:S(2)}) async-start(bf16[8,2,65536]{2,1,0:T(2,128)(2,1)} %broadcast_select_fusion), calls=%async_computation | async-start | bytes 4194304 | tf_op jit(solution)/shard_map/all_to_all | solution.py:117
  317.4 3.5 collective-permute-start.3
  324.2 39.5 %collective-permute-done.3 = bf16[256,256]{1,0:T(8,128)(2,1)S(1)} collective-permute-done((bf16[256,256]{1,0:T(8,128)(2,1)S(1)}, bf16[256,256]{1,0:T(8,128)(2,1)S(1)}, u32[]{:S(2)}, u32[]{:S(2)}) %collective-permute-start.3) | collective-permute-done | bytes 131104 | tf_op jit(solution)/shard_map/ppermute | solution.py:16
  364.3 11.3 %fusion.69 = (f32[16,256]{1,0:T(8,128)}, bf16[16,256,1024]{1,2,0:T(8,128)(2,1)}) fusion(pred[256,1024]{0,1:T(8,128)(4,1)S(1)} %pad_add_fusion, bf16[256,2,16,128]{0,3,2,1:T(8,128)(2,1)} %bitcast.118, bf16[256,128]{1,0:T(8,128)(2,1)S(1)} %get-tuple-element.30, bf16[256,128]{1,0:T(8,128)(2,1)S(1)} %get-tuple-element.28, ...), kind=kOutput, calls=%fused_computation.121 | convolution fusion | flops 1099957248 | bytes 10240000 | tf_op jit(solution)/shard_map/sub | solution.py:90
  375.6 4.8 %fusion.24 = bf16[256,1,16,128]{0,3,2,1:T(8,128)(2,1)S(1)} fusion(bf16[16,256,1024]{1,2,0:T(8,128)(2,1)} %get-tuple-element.39, f32[256,16]{0,1:T(8,128)} %bitcast.130, bf16[256,128]{1,0:T(8,128)(2,1)} %get-tuple-element.22, bf16[256,128]{1,0:T(8,128)(2,1)} %get-tuple-element.20, bf16[256,128]{1,0:T(8,128)(2,1)} %get-tuple-element.18, ...), kind=kOutput, calls=%fused_computation.27 | convolution fusion | flops 1075838976 | bytes 9715712 | tf_op jit(solution)/shard_map/qts,sd->tqd/dot_general | solution.py:93
  380.4 11.3 %fusion.68 = (f32[16,256]{1,0:T(8,128)}, bf16[16,256,1024]{1,2,0:T(8,128)(2,1)}) fusion(pred[256,1024]{0,1:T(8,128)(4,1)S(1)} %pad_add_fusion, bf16[256,2,16,128]{0,3,2,1:T(8,128)(2,1)} %bitcast.119, bf16[256,128]{1,0:T(8,128)(2,1)} %get-tuple-element.31, bf16[256,128]{1,0:T(8,128)(2,1)} %get-tuple-element.29, bf16[256,128]{1,0:T(8,128)(2,1)} %get-tuple-element.27, ...), kind=kOutput, calls=%fused_computation.120 | convolution fusion | flops 1099957248 | bytes 10240000 | tf_op jit(solution)/shard_map/sub | solution.py:90
  391.7 4.8 %fusion.27 = bf16[256,1,16,128]{0,3,2,1:T(8,128)(2,1)S(1)} fusion(bf16[16,256,1024]{1,2,0:T(8,128)(2,1)} %get-tuple-element.37, f32[256,16]{0,1:T(8,128)} %bitcast.129, bf16[256,128]{1,0:T(8,128)(2,1)S(1)} %copy-done, bf16[256,128]{1,0:T(8,128)(2,1)} %get-tuple-element.21, bf16[256,128]{1,0:T(8,128)(2,1)} %get-tuple-element.19, ...), kind=kOutput, calls=%fused_computation.28 | convolution fusion | flops 1075838976 | bytes 9715712 | tf_op jit(solution)/shard_map/qts,sd->tqd/dot_general | solution.py:93
  396.5 1.5 pad_maximum_fusion
  398.0 4.1 copy.32
  402.1 1.9 reshape.228
  403.9 2.0 convolution_convert_fusion
  405.9 1.1 copy.42
  (49 shorter events, 8.3 us)
Async XLA Ops:
  7.2 6.3 %copy-start.2 = (s32[8]{0:T(128)S(1)}, s32[8]{0:T(128)}, u32[]{:S(2)}) copy-start(s32[8]{0:T(128)} %param.10) | copy-start | bytes 100
  7.2 6.8 %copy-start.1 = (s32[8]{0:T(128)S(1)}, s32[8]{0:T(128)}, u32[]{:S(2)}) copy-start(s32[8]{0:T(128)} %param.11) | copy-start | bytes 100
  7.2 23.6 %all-gather.4.cloned.1.call-start = ((), (), s32[]{:S(2)}) async-start(), calls=%async_computation.1 | async-start | bytes 12582912 | tf_op jit(solution)/shard_map/all_gather | solution.py:51
  7.9 148.1 %all-gather.6.cloned.1.call-start = ((), (), s32[]{:S(2)}) async-start(), calls=%async_computation.2 | async-start | bytes 9437184 | tf_op jit(solution)/shard_map/all_gather | solution.py:59
  8.7 283.7 %all-gather.8.cloned.1.call-start = ((), (), s32[]{:S(2)}) async-start(), calls=%async_computation.3 | async-start | bytes 9437184 | tf_op jit(solution)/shard_map/all_gather | solution.py:54
  164.1 153.2 %collective-permute-start.2 = (bf16[256,256]{1,0:T(8,128)(2,1)S(1)}, bf16[256,256]{1,0:T(8,128)(2,1)S(1)}, u32[]{:S(2)}, u32[]{:S(2)}) collective-permute-start(bf16[256,256]{1,0:T(8,128)(2,1)S(1)} %convolution_convert_fusion.2), channel_id=1, source_target_pairs={{0,6},{2,8},{4,10},{6,12},{8,14},{1,7},{3,9},{5,11},{7,13},{9,15},... | collective-permute-start | bytes 393224 | tf_op jit(solution)/shard_map/ppermute | solution.py:16
  169.3 152.3 %collective-permute-start.1 = (bf16[256,256]{1,0:T(8,128)(2,1)S(1)}, bf16[256,256]{1,0:T(8,128)(2,1)S(1)}, u32[]{:S(2)}, u32[]{:S(2)}) collective-permute-start(bf16[256,256]{1,0:T(8,128)(2,1)S(1)} %convolution_convert_fusion.2), channel_id=1, source_target_pairs={{0,4},{2,6},{4,8},{6,10},{8,12},{10,14},{1,5},{3,7},{5,9},{7,11},{... | collective-permute-start | bytes 393224 | tf_op jit(solution)/shard_map/ppermute | solution.py:16
  171.2 151.0 %collective-permute-start = (bf16[256,256]{1,0:T(8,128)(2,1)S(1)}, bf16[256,256]{1,0:T(8,128)(2,1)S(1)}, u32[]{:S(2)}, u32[]{:S(2)}) collective-permute-start(bf16[256,256]{1,0:T(8,128)(2,1)S(1)} %convolution_convert_fusion.2), channel_id=1, source_target_pairs={{0,2},{2,4},{4,6},{6,8},{8,10},{10,12},{12,14},{1,3},{3,5},{5,7},{... | collective-permute-start | bytes 393224 | tf_op jit(solution)/shard_map/ppermute | solution.py:16
  300.4 22.5 %collective-permute-start.5 = (bf16[256,256]{1,0:T(8,128)(2,1)S(1)}, bf16[256,256]{1,0:T(8,128)(2,1)S(1)}, u32[]{:S(2)}, u32[]{:S(2)}) collective-permute-start(bf16[256,256]{1,0:T(8,128)(2,1)S(1)} %convolution_convert_fusion.1), channel_id=1, source_target_pairs={{0,6},{2,8},{4,10},{6,12},{8,14},{1,7},{3,9},{5,11},{7,13},{9,15},... | collective-permute-start | bytes 393224 | tf_op jit(solution)/shard_map/ppermute | solution.py:16
  305.6 18.0 %collective-permute-start.4 = (bf16[256,256]{1,0:T(8,128)(2,1)S(1)}, bf16[256,256]{1,0:T(8,128)(2,1)S(1)}, u32[]{:S(2)}, u32[]{:S(2)}) collective-permute-start(bf16[256,256]{1,0:T(8,128)(2,1)S(1)} %convolution_convert_fusion.1), channel_id=1, source_target_pairs={{0,4},{2,6},{4,8},{6,10},{8,12},{10,14},{1,5},{3,7},{5,9},{7,11},{... | collective-permute-start | bytes 393224 | tf_op jit(solution)/shard_map/ppermute | solution.py:16
  311.1 91.0 %all-to-all-start = ((bf16[8,2,65536]{2,1,0:T(2,128)(2,1)}), bf16[8,2,65536]{2,1,0:T(2,128)(2,1)S(1)}, u32[]{:S(2)}, u32[]{:S(2)}) async-start(bf16[8,2,65536]{2,1,0:T(2,128)(2,1)} %broadcast_select_fusion), calls=%async_computation | async-start | bytes 4194304 | tf_op jit(solution)/shard_map/all_to_all | solution.py:117
  317.4 46.3 %collective-permute-start.3 = (bf16[256,256]{1,0:T(8,128)(2,1)S(1)}, bf16[256,256]{1,0:T(8,128)(2,1)S(1)}, u32[]{:S(2)}, u32[]{:S(2)}) collective-permute-start(bf16[256,256]{1,0:T(8,128)(2,1)S(1)} %convolution_convert_fusion.1), channel_id=1, source_target_pairs={{0,2},{2,4},{4,6},{6,8},{8,10},{10,12},{12,14},{1,3},{3,5},{5,7},{... | collective-permute-start | bytes 393224 | tf_op jit(solution)/shard_map/ppermute | solution.py:16
  380.4 11.4 %copy-start = (bf16[256,128]{1,0:T(8,128)(2,1)S(1)}, bf16[256,128]{1,0:T(8,128)(2,1)}, u32[]{:S(2)}) copy-start(bf16[256,128]{1,0:T(8,128)(2,1)} %get-tuple-element.23) | copy-start | bytes 196612
Sparse Core Ops, SparseCore 0:
  9.6 21.1 all-gather.3
  32.9 123.0 all-gather.5
  158.2 134.1 all-gather.7
where the time goes:
time: 416 us; the launch traced here: 414 us
  waiting for transfers between devices  301 us (72%)
  matrix products  50.3 us (12%)
  starting transfers between devices  25.9 us (6%)
  local copies, waits for them, and re-layouts  15.9 us (4%)
  between operations  14 us (3%)
  other arithmetic  6.09 us (1%)
    all_gather x1, waiting for transfers between devices, per_device(): lax.all_gather(w_value, 'fsdp', axis=0, tiled=True)  125 us
    all_gather x1, waiting for transfers between devices, per_device(): lax.all_gather(w_key, 'fsdp', axis=0, tiled=True)  119 us
    ppermute x6, waiting for transfers between devices, shifted(): return lax.ppermute(array, axis, pairs)  39.5 us
    sub x2, matrix products, per_device(): expo = jnp.where(visible[None], jnp.exp(scores - row_top), 0.0)  22.6 us
    ppermute x6, starting transfers between devices, shifted(): return lax.ppermute(array, axis, pairs)  20.1 us
    all_gather x1, waiting for transfers between devices, per_device(): full_rows = lax.all_gather(activations, 'head', axis=1, tiled=True)  15.9 us
    unnamed x10, local copies, waits for them, and re-layouts  9.54 us
    dot_general x2, matrix products, per_device(): jnp.einsum('qts,sd->tqd', weights, value_head, preferred_element_type=jnp...  9.5 us
  transfers between devices with their start and end apart: 10, of which 4 were waited for; matrix products, arithmetic and copies ran while one was open for 16% of the time, Pallas kernels for 0%

commit v1 on v0

--- a/solution.py
+++ b/solution.py
@@ -8,10 +8,12 @@
 HD = 128
 PAGE = 128
 SPAN = 3
+FSDP = ("z", "y")
+PLANE = ("groups", "y")
 
 
 def shifted(array, axis, by):
-    count = lax.axis_size(axis)
+    count = lax.axis_size("z") * lax.axis_size("y")
     pairs = [(i, i + by) for i in range(count) if 0 <= i + by < count]
     return lax.ppermute(array, axis, pairs)
 
@@ -32,6 +34,27 @@
     return owner_dev * cache_pages + global_pages - doc_begin
 
 
+def project(activations, w_key, w_value):
+    tok_rows, half = activations.shape
+    n_groups, n_y = lax.axis_size("groups"), lax.axis_size("y")
+    depth, width = w_key.shape
+    part = depth // n_groups
+    n_z = half // (part * n_y * n_groups)
+    split = activations.reshape(tok_rows, n_z, n_y, n_groups, part)
+    split = jnp.transpose(split, (3, 2, 0, 1, 4)).reshape(n_groups * n_y, tok_rows, n_z * part)
+    mine = lax.all_to_all(split, PLANE, split_axis=0, concat_axis=0, tiled=True)
+    mine = mine.reshape(n_groups * n_y * tok_rows, n_z * part)
+    both = lax.all_gather(mine, "head", axis=1, tiled=True)
+    group = lax.axis_index("groups")
+    weights = jnp.concatenate([w_key, w_value], axis=1)
+    weights = lax.dynamic_slice(weights, (group * part, 0), (part, 2 * width))
+    weights = lax.all_gather(weights, "z", axis=0, tiled=True)
+    partial = jnp.dot(both, weights, preferred_element_type=jnp.float32)
+    rows = lax.psum_scatter(partial, PLANE, scatter_dimension=0, tiled=True)
+    rows = rows.astype(jnp.bfloat16)
+    return rows[:, :width], rows[:, width:]
+
+
 def masked_scores(query_head, key_head, visible, score_scale):
     scores = (
         jnp.einsum("tqd,sd->qts", query_head, key_head, preferred_element_type=jnp.float32)
@@ -45,29 +68,17 @@
     width_kv = w_key.shape[1]
     kv_here = width_kv // HD
     per_group = QH // KVH
-    n_dev = lax.axis_size("fsdp")
-    my_index = lax.axis_index("fsdp")
+    n_dev = lax.axis_size("z") * lax.axis_size("y")
+    my_index = lax.axis_index(FSDP)
     score_scale = HD ** (-0.5)
-    full_rows = lax.all_gather(activations, "head", axis=1, tiled=True)
-    key_sum = jnp.dot(
-        full_rows,
-        lax.all_gather(w_key, "fsdp", axis=0, tiled=True),
-        preferred_element_type=jnp.float32,
-    )
-    value_sum = jnp.dot(
-        full_rows,
-        lax.all_gather(w_value, "fsdp", axis=0, tiled=True),
-        preferred_element_type=jnp.float32,
-    )
-    key_rows = key_sum.astype(jnp.bfloat16)
-    value_rows = value_sum.astype(jnp.bfloat16)
+    key_rows, value_rows = project(activations, w_key, w_value)
     doc_ends = jnp.cumsum(request_pages)
     doc_begins = doc_ends - request_pages
     first_tok = my_index * tok_rows
     query_docs, query_pos = token_docs(first_tok, tok_rows, doc_ends)
     blocks = [(key_rows, value_rows, first_tok)]
     for distance in range(1, SPAN + 1):
-        near_k, near_v = shifted((key_rows, value_rows), "fsdp", distance)
+        near_k, near_v = shifted((key_rows, value_rows), FSDP, distance)
         blocks.append((near_k, near_v, first_tok - distance * tok_rows))
     described = []
     for index, (block_k, block_v, block_first) in enumerate(blocks):
@@ -114,7 +125,7 @@
     target = page_slot(own_pages, doc_ends, doc_begins, request_owner, cache_pages) // cache_pages
     routed = target[None, :] == jnp.arange(n_dev, dtype=jnp.int32)[:, None]
     outgoing = jnp.where(routed[:, :, None], flat_pages[None], jnp.zeros((), jnp.bfloat16))
-    incoming = lax.all_to_all(outgoing, "fsdp", split_axis=0, concat_axis=0, tiled=True)
+    incoming = lax.all_to_all(outgoing, FSDP, split_axis=0, concat_axis=0, tiled=True)
     incoming = incoming.reshape(n_dev * pages_here, 2 * PAGE * width_kv)
     source_pages = jnp.arange(n_dev * pages_here, dtype=jnp.int32)
     local_slot = (
@@ -128,17 +139,23 @@
 
 
 def solution(mesh):
+    groups, fsdp, head = mesh.devices.shape
+    n_y = max(1, 4 // groups)
+    fine = jax.sharding.Mesh(
+        mesh.devices.reshape(groups, fsdp // n_y, n_y, head), ("groups", "z", "y", "head")
+    )
+    tokens = ("groups", "z", "y")
     return jax.shard_map(
         per_device,
-        mesh=mesh,
+        mesh=fine,
         in_specs=(
-            P(("groups", "fsdp"), "head"),
-            P(("groups", "fsdp"), "head"),
-            P("fsdp", "head"),
-            P("fsdp", "head"),
+            P(tokens, "head"),
+            P(tokens, "head"),
+            P(FSDP, "head"),
+            P(FSDP, "head"),
             P("groups"),
             P("groups"),
         ),
-        out_specs=(P(("groups", "fsdp"), "head"), P(("groups", "fsdp"), None, None, "head")),
+        out_specs=(P(tokens, "head"), P(tokens, None, None, "head")),
         check_vma=False,
     )

time: 416 us -> 286 us (0.69)
  waiting for transfers between devices: 301 us -> 111 us
  blocking collectives: 0 us -> 50 us
  local copies, waits for them, and re-layouts: 15.9 us -> 29.2 us
  matrix products: 50.3 us -> 45 us
    all_gather x3 -> x2, waiting for transfers between devices: 260 us -> 37.5 us  [the longest x1 22.7 us: project(): both = lax.all_gather(mine, 'head', axis=1, tiled=True)]
    all_to_all x0 -> x1, blocking collectives: none -> 50 us  [project(): mine = lax.all_to_all(split, PLANE, split_axis=0, concat_axis=0, tiled=True)]
    reduce_scatter x0 -> x1, waiting for transfers between devices: none -> 31.5 us  [project(): rows = lax.psum_scatter(partial, PLANE, scatter_dimension=0, tiled=True)]
    all_to_all x0 -> x1, local copies, waits for them, and re-layouts: none -> 6.27 us  [project(): mine = lax.all_to_all(split, PLANE, split_axis=0, concat_axis=0, tiled=True)]
    dot_general x2 -> x1, matrix products: 16.2 us -> 10.6 us  [project(): partial = jnp.dot(both, weights, preferred_element_type=jnp.float32)]
    unnamed x10 -> x13, local copies, waits for them, and re-layouts: 9.54 us -> 14.3 us
  transfers between devices with their start and end apart: 10 -> 10, of which waited for: 4 -> 4; matrix products, arithmetic and copies ran while one was open for 16% -> 23% of each run, Pallas kernels for 0% -> 0%
where the time goes in v1:
time: 286 us; the launch traced here: 283 us
  waiting for transfers between devices  111 us (39%)
  blocking collectives  50 us (17%)
  matrix products  45 us (16%)
  local copies, waits for them, and re-layouts  29.2 us (10%)
  starting transfers between devices  25 us (9%)
  between operations  14 us (5%)
  other arithmetic  9.4 us (3%)
    all_to_all x1, blocking collectives, project(): mine = lax.all_to_all(split, PLANE, split_axis=0, concat_axis=0, tiled=True)  50 us
    ppermute x6, waiting for transfers between devices, shifted(): return lax.ppermute(array, axis, pairs)  41.8 us
    reduce_scatter x1, waiting for transfers between devices, project(): rows = lax.psum_scatter(partial, PLANE, scatter_dimension=0, tiled=True)  31.5 us
    sub x2, matrix products, per_device(): expo = jnp.where(visible[None], jnp.exp(scores - row_top), 0.0)  22.7 us
    all_gather x1, waiting for transfers between devices, project(): both = lax.all_gather(mine, 'head', axis=1, tiled=True)  22.7 us
    ppermute x6, starting transfers between devices, shifted(): return lax.ppermute(array, axis, pairs)  18.5 us
    all_gather x1, waiting for transfers between devices, project(): weights = lax.all_gather(weights, 'z', axis=0, tiled=True)  14.8 us
    unnamed x13, local copies, waits for them, and re-layouts  14.3 us
  transfers between devices with their start and end apart: 10, of which 4 were waited for; matrix products, arithmetic and copies ran while one was open for 23% of the time, Pallas kernels for 0%

profile of v1, /device:TPU:14, one launch (start us, length us, event | category | flops | bytes accessed | tf_op | source)
XLA Modules:
  0.0 283.3 jit_solution(8302556152086442075)
XLA Ops:
  7.2 2.2 fusion.30
  9.5 6.4 %copy.36 = bf16[256,8192]{0,1:T(8,128)(2,1)} copy(bf16[256,8192]{1,0:T(8,128)(2,1)} %param.6) | data formatting | bytes 8388608 | tf_op args[0]
  15.9 2.5 copy.37
  18.5 50.0 %all_to_all.10 = bf16[4,256,2048]{1,2,0:T(8,128)(2,1)} all-to-all(bf16[4,256,2048]{1,2,0:T(8,128)(2,1)S(1)} %bitcast.118), channel_id=1, replica_groups=mesh['groups'=2,'z'=4,'y'=2,'head'=2] {'groups','y'}, dimensions={0} | all-to-all | bytes 8388608 | tf_op jit(solution)/shard_map/all_to_all | solution.py:45
  68.4 6.3 %copy.38 = bf16[4,256,2048]{2,1,0:T(8,128)(2,1)} copy(bf16[4,256,2048]{1,2,0:T(8,128)(2,1)} %all_to_all.10) | data formatting | bytes 8388608 | tf_op jit(solution)/shard_map/all_to_all | solution.py:45
  74.8 14.8 %all-gather.3.cloned.1.call-done = bf16[4096,512]{1,0:T(8,128)(2,1)} async-done(((bf16[1024,512]{1,0:T(8,128)(2,1)}), bf16[4096,512]{1,0:T(8,128)(2,1)}) %all-gather.3.cloned.1.call-update) | async-done | bytes 4194320 | tf_op jit(solution)/shard_map/all_gather | solution.py:51
  89.6 22.7 %all-gather.5.cloned.1.call-done = bf16[1024,4096]{1,0:T(8,128)(2,1)} async-done(((bf16[1024,2048]{1,0:T(8,128)(2,1)}), bf16[1024,4096]{1,0:T(8,128)(2,1)}) %all-gather.5.cloned.1.call-update) | async-done | bytes 8388624 | tf_op jit(solution)/shard_map/all_gather | solution.py:47
  112.2 10.6 %convolution_bitcast_fusion = f32[1024,512]{0,1:T(8,128)} fusion(bf16[4096,512]{1,0:T(8,128)(2,1)} %all-gather.3.cloned.1.call-done, bf16[1024,4096]{1,0:T(8,128)(2,1)} %all-gather.5.cloned.1.call-done), kind=kOutput, calls=%fused_computation.29 | convolution fusion | flops 4294967296 | bytes 14680064 | tf_op jit(solution)/shard_map/dot_general | solution.py:52
  123.0 2.4 copy.39
  126.7 31.5 %reduce-scatter.2.cloned.1.call-done = f32[256,512]{0,1:T(8,128)} async-done(((f32[1024,512]{0,1:T(8,128)}), f32[256,512]{0,1:T(8,128)}) %reduce-scatter.2.cloned.1.call-update) | async-done | bytes 524304 | tf_op jit(solution)/shard_map/reduce_scatter | solution.py:53
  159.3 4.3 %collective-permute-start.3 = (bf16[256,256]{0,1:T(8,128)(2,1)S(1)}, bf16[256,256]{0,1:T(8,128)(2,1)S(1)}, u32[]{:S(2)}, u32[]{:S(2)}) collective-permute-start(bf16[256,256]{0,1:T(8,128)(2,1)S(1)} %get-tuple-element.23), channel_id=1, source_target_pairs={{0,2},{2,4},{4,6},{6,8},{8,10},{10,12},{12,14},{1,3},{3,5},{5,7},{... | collective-permute-start | bytes 393224 | tf_op jit(solution)/shard_map/ppermute | solution.py:18
  163.6 3.4 %collective-permute-start.4 = (bf16[256,256]{0,1:T(8,128)(2,1)S(1)}, bf16[256,256]{0,1:T(8,128)(2,1)S(1)}, u32[]{:S(2)}, u32[]{:S(2)}) collective-permute-start(bf16[256,256]{0,1:T(8,128)(2,1)S(1)} %get-tuple-element.23), channel_id=1, source_target_pairs={{0,4},{2,6},{4,8},{6,10},{8,12},{10,14},{1,5},{3,7},{5,9},{7,11},{... | collective-permute-start | bytes 393224 | tf_op jit(solution)/shard_map/ppermute | solution.py:18
  168.9 2.5 collective-permute-start
  171.4 1.9 collective-permute-start.1
  173.9 3.2 %broadcast_select_fusion = bf16[8,2,65536]{2,1,0:T(2,128)(2,1)} fusion(pred[8,2]{1,0:T(8,128)(4,1)S(1)} %iota_compare_fusion, bf16[2,65536]{1,0:T(2,128)(2,1)S(1)} %bitcast.124), kind=kLoop, calls=%fused_computation.19 | loop fusion | flops 1048576 | bytes 2359312 | tf_op jit(solution)/shard_map/jit(_where)/select_n | solution.py:127
  177.1 6.4 %all-to-all-start.1 = ((bf16[8,2,65536]{2,1,0:T(2,128)(2,1)}), bf16[8,2,65536]{2,1,0:T(2,128)(2,1)S(1)}, u32[]{:S(2)}, u32[]{:S(2)}) async-start(bf16[8,2,65536]{2,1,0:T(2,128)(2,1)} %broadcast_select_fusion), calls=%async_computation.2 | async-start | bytes 4194304 | tf_op jit(solution)/shard_map/all_to_all | solution.py:128
  184.2 4.5 %collective-permute-start.2 = (bf16[256,256]{0,1:T(8,128)(2,1)S(1)}, bf16[256,256]{0,1:T(8,128)(2,1)S(1)}, u32[]{:S(2)}, u32[]{:S(2)}) collective-permute-start(bf16[256,256]{0,1:T(8,128)(2,1)S(1)} %get-tuple-element.22), channel_id=1, source_target_pairs={{0,6},{2,8},{4,10},{6,12},{8,14},{1,7},{3,9},{5,11},{7,13},{9,15},... | collective-permute-start | bytes 393224 | tf_op jit(solution)/shard_map/ppermute | solution.py:18
  191.3 41.8 %collective-permute-done.2 = bf16[256,256]{0,1:T(8,128)(2,1)S(1)} collective-permute-done((bf16[256,256]{0,1:T(8,128)(2,1)S(1)}, bf16[256,256]{0,1:T(8,128)(2,1)S(1)}, u32[]{:S(2)}, u32[]{:S(2)}) %collective-permute-start.2) | collective-permute-done | bytes 131104 | tf_op jit(solution)/shard_map/ppermute | solution.py:18
  233.8 11.4 %fusion.70 = (f32[16,256]{1,0:T(8,128)}, bf16[16,256,1024]{1,2,0:T(8,128)(2,1)}) fusion(pred[256,1024]{0,1:T(8,128)(4,1)S(1)} %pad_add_fusion, bf16[256,2,16,128]{0,3,2,1:T(8,128)(2,1)} %bitcast.122, bf16[256,128]{0,1:T(8,128)(2,1)S(1)} %get-tuple-element.34, bf16[256,128]{0,1:T(8,128)(2,1)S(1)} %get-tuple-element.32, ...), kind=kOutput, calls=%fused_computation.123 | convolution fusion | flops 1099957248 | bytes 10240000 | tf_op jit(solution)/shard_map/sub | solution.py:101
  245.1 4.8 %fusion.24 = bf16[256,1,16,128]{0,3,2,1:T(8,128)(2,1)S(1)} fusion(bf16[16,256,1024]{1,2,0:T(8,128)(2,1)} %get-tuple-element.43, f32[256,16]{0,1:T(8,128)} %bitcast.134, bf16[256,128]{0,1:T(8,128)(2,1)} %get-tuple-element.28, bf16[256,128]{0,1:T(8,128)(2,1)} %get-tuple-element.26, bf16[256,128]{0,1:T(8,128)(2,1)} %get-tuple-element.24, ...), kind=kOutput, calls=%fused_computation.30 | convolution fusion | flops 1075838976 | bytes 9715712 | tf_op jit(solution)/shard_map/qts,sd->tqd/dot_general | solution.py:104
  250.0 11.4 %fusion.69 = (f32[16,256]{1,0:T(8,128)}, bf16[16,256,1024]{1,2,0:T(8,128)(2,1)}) fusion(pred[256,1024]{0,1:T(8,128)(4,1)S(1)} %pad_add_fusion, bf16[256,2,16,128]{0,3,2,1:T(8,128)(2,1)} %bitcast.123, bf16[256,128]{0,1:T(8,128)(2,1)} %get-tuple-element.35, bf16[256,128]{0,1:T(8,128)(2,1)S(1)} %get-tuple-element.33, bf16[256,128]{0,1:T(8,128)(2,1)S(1)} %copy-done.1, ...), kind=kOutput, calls=%fused_computation.122 | convolution fusion | flops 1099957248 | bytes 10240000 | tf_op jit(solution)/shard_map/sub | solution.py:101
  261.4 4.8 %fusion.27 = bf16[256,1,16,128]{0,3,2,1:T(8,128)(2,1)S(1)} fusion(bf16[16,256,1024]{1,2,0:T(8,128)(2,1)} %get-tuple-element.41, f32[256,16]{0,1:T(8,128)} %bitcast.133, bf16[256,128]{0,1:T(8,128)(2,1)} %get-tuple-element.29, bf16[256,128]{0,1:T(8,128)(2,1)} %get-tuple-element.27, bf16[256,128]{0,1:T(8,128)(2,1)} %get-tuple-element.25, ...), kind=kOutput, calls=%fused_computation.31 | convolution fusion | flops 1075838976 | bytes 9715712 | tf_op jit(solution)/shard_map/qts,sd->tqd/dot_general | solution.py:104
  267.7 4.1 %copy.48 = bf16[256,4096]{1,0:T(8,128)(2,1)} copy(bf16[256,4096]{0,1:T(8,128)(2,1)} %bitcast.120) | data formatting | bytes 4194304
  273.6 2.0 convolution_convert_fusion
  (58 shorter events, 13.5 us)
Async XLA Ops:
  7.2 82.4 %all-gather.3.cloned.1.call-start = ((), (), s32[]{:S(2)}) async-start(), calls=%async_computation.3 | async-start | bytes 5242880 | tf_op jit(solution)/shard_map/all_gather | solution.py:51
  9.5 102.8 %all-gather.5.cloned.1.call-start = ((), (), s32[]{:S(2)}) async-start(), calls=%async_computation.4 | async-start | bytes 12582912 | tf_op jit(solution)/shard_map/all_gather | solution.py:47
  74.7 48.1 %copy-start.3 = (s32[8]{0:T(128)S(1)}, s32[8]{0:T(128)}, u32[]{:S(2)}) copy-start(s32[8]{0:T(128)} %param.10) | copy-start | bytes 100
  74.7 48.3 %copy-start = (bf16[256,4096]{1,0:T(8,128)(2,1)S(1)}, bf16[256,4096]{1,0:T(8,128)(2,1)}, u32[]{:S(2)}) copy-start(bf16[256,4096]{1,0:T(8,128)(2,1)} %param.7) | copy-start | bytes 6291460
  74.7 83.5 %reduce-scatter.2.cloned.1.call-start = ((), (), s32[]{:S(2)}) async-start(), calls=%async_computation.5 | async-start | bytes 2621440 | tf_op jit(solution)/shard_map/reduce_scatter | solution.py:53
  122.8 3.0 %copy-start.2 = (s32[8]{0:T(128)S(1)}, s32[8]{0:T(128)}, u32[]{:S(2)}) copy-start(s32[8]{0:T(128)} %param.11) | copy-start | bytes 100
  159.3 24.9 %collective-permute-start.3 = (bf16[256,256]{0,1:T(8,128)(2,1)S(1)}, bf16[256,256]{0,1:T(8,128)(2,1)S(1)}, u32[]{:S(2)}, u32[]{:S(2)}) collective-permute-start(bf16[256,256]{0,1:T(8,128)(2,1)S(1)} %get-tuple-element.23), channel_id=1, source_target_pairs={{0,2},{2,4},{4,6},{6,8},{8,10},{10,12},{12,14},{1,3},{3,5},{5,7},{... | collective-permute-start | bytes 393224 | tf_op jit(solution)/shard_map/ppermute | solution.py:18
  163.6 25.8 %collective-permute-start.4 = (bf16[256,256]{0,1:T(8,128)(2,1)S(1)}, bf16[256,256]{0,1:T(8,128)(2,1)S(1)}, u32[]{:S(2)}, u32[]{:S(2)}) collective-permute-start(bf16[256,256]{0,1:T(8,128)(2,1)S(1)} %get-tuple-element.23), channel_id=1, source_target_pairs={{0,4},{2,6},{4,8},{6,10},{8,12},{10,14},{1,5},{3,7},{5,9},{7,11},{... | collective-permute-start | bytes 393224 | tf_op jit(solution)/shard_map/ppermute | solution.py:18
  167.0 22.4 %collective-permute-start.5 = (bf16[256,256]{0,1:T(8,128)(2,1)S(1)}, bf16[256,256]{0,1:T(8,128)(2,1)S(1)}, u32[]{:S(2)}, u32[]{:S(2)}) collective-permute-start(bf16[256,256]{0,1:T(8,128)(2,1)S(1)} %get-tuple-element.23), channel_id=1, source_target_pairs={{0,6},{2,8},{4,10},{6,12},{8,14},{1,7},{3,9},{5,11},{7,13},{9,15},... | collective-permute-start | bytes 393224 | tf_op jit(solution)/shard_map/ppermute | solution.py:18
  168.9 21.1 %collective-permute-start = (bf16[256,256]{0,1:T(8,128)(2,1)S(1)}, bf16[256,256]{0,1:T(8,128)(2,1)S(1)}, u32[]{:S(2)}, u32[]{:S(2)}) collective-permute-start(bf16[256,256]{0,1:T(8,128)(2,1)S(1)} %get-tuple-element.22), channel_id=1, source_target_pairs={{0,2},{2,4},{4,6},{6,8},{8,10},{10,12},{12,14},{1,3},{3,5},{5,7},{... | collective-permute-start | bytes 393224 | tf_op jit(solution)/shard_map/ppermute | solution.py:18
  171.4 19.2 %collective-permute-start.1 = (bf16[256,256]{0,1:T(8,128)(2,1)S(1)}, bf16[256,256]{0,1:T(8,128)(2,1)S(1)}, u32[]{:S(2)}, u32[]{:S(2)}) collective-permute-start(bf16[256,256]{0,1:T(8,128)(2,1)S(1)} %get-tuple-element.22), channel_id=1, source_target_pairs={{0,4},{2,6},{4,8},{6,10},{8,12},{10,14},{1,5},{3,7},{5,9},{7,11},{... | collective-permute-start | bytes 393224 | tf_op jit(solution)/shard_map/ppermute | solution.py:18
  177.1 94.7 %all-to-all-start.1 = ((bf16[8,2,65536]{2,1,0:T(2,128)(2,1)}), bf16[8,2,65536]{2,1,0:T(2,128)(2,1)S(1)}, u32[]{:S(2)}, u32[]{:S(2)}) async-start(bf16[8,2,65536]{2,1,0:T(2,128)(2,1)} %broadcast_select_fusion), calls=%async_computation.2 | async-start | bytes 4194304 | tf_op jit(solution)/shard_map/all_to_all | solution.py:128
  184.2 48.9 %collective-permute-start.2 = (bf16[256,256]{0,1:T(8,128)(2,1)S(1)}, bf16[256,256]{0,1:T(8,128)(2,1)S(1)}, u32[]{:S(2)}, u32[]{:S(2)}) collective-permute-start(bf16[256,256]{0,1:T(8,128)(2,1)S(1)} %get-tuple-element.22), channel_id=1, source_target_pairs={{0,6},{2,8},{4,10},{6,12},{8,14},{1,7},{3,9},{5,11},{7,13},{9,15},... | collective-permute-start | bytes 393224 | tf_op jit(solution)/shard_map/ppermute | solution.py:18
  245.1 4.9 %copy-start.1 = (bf16[256,128]{0,1:T(8,128)(2,1)S(1)}, bf16[256,128]{0,1:T(8,128)(2,1)}, u32[]{:S(2)}) copy-start(bf16[256,128]{0,1:T(8,128)(2,1)} %get-tuple-element.31) | copy-start | bytes 196612
Sparse Core Ops, SparseCore 0:
  10.1 79.3 all-gather.2
  91.1 21.0 all-gather.4
  123.0 35.1 reduce-scatter.1

commit v2 on v0

v2 whole, which is shorter than its diff:
```python
import functools
import jax
import jax.numpy as jnp
from jax import lax
from jax.experimental import pallas as pl
from jax.experimental.pallas import tpu as pltpu
from jax.sharding import PartitionSpec as P

QH = 64
KVH = 4
HD = 128
PAGE = 128
SPAN = 3
PLANE = 4


def rows_kernel(
    n_groups, n_z, n_y, acts, w_key, w_value, out, abuf, wbuf, acc, sbuf, rbuf, gbuf,
    w_right, w_left, w_recv, a_send, a_recv, f_send, f_recv, r_send, r_recv,
    g_right, g_left, g_cross, g_recv, c_recv, loc_w, loc_a, loc_out,
):
    group = lax.axis_index("groups")
    fsdp = lax.axis_index("fsdp")
    head = lax.axis_index("head")
    z = fsdp // n_y
    y = fsdp % n_y
    me = group * n_y + y
    rows = acts.shape[0]
    part = w_key.shape[0] // n_groups
    width = w_key.shape[1]
    half_z = n_z // 2
    sibling = (group, fsdp, 1 - head)
    right = (group, fsdp + n_y, head)
    left = (group, fsdp - n_y, head)
    has_right = z < n_z - 1
    has_left = z > 0

    def chip(p):
        return (p // n_y, z * n_y + p % n_y, head)

    def remote(src, dst, send, recv, dev):
        return pltpu.make_async_remote_copy(
            src_ref=src, dst_ref=dst, send_sem=send, recv_sem=recv,
            device_id=dev, device_id_type=pl.DeviceIdType.MESH,
        )

    barrier = pltpu.get_barrier_semaphore()

    def greet(dev):
        pl.semaphore_signal(barrier, inc=1, device_id=dev, device_id_type=pl.DeviceIdType.MESH)

    for j in range(1, PLANE):
        greet(chip((me + j) % PLANE))
    greet(sibling)
    pl.when(has_right)(lambda: greet(right))
    pl.when(has_left)(lambda: greet(left))
    pl.semaphore_wait(barrier, PLANE + jnp.minimum(z, 1) + jnp.minimum(n_z - 1 - z, 1))

    mine = pl.ds(pl.multiple_of(group * part, part), part)
    w_own = [w_key.at[mine, :], w_value.at[mine, :]]

    def w_copy(block, c, dev, send, own):
        src = w_own[c] if own else wbuf.at[block, c]
        return remote(src, wbuf.at[block, c], send.at[block, c], w_recv.at[block, c], dev)

    for c in range(2):
        pl.when(has_right)(lambda c=c: w_copy(z, c, right, w_right, True).start())
        pl.when(has_left)(lambda c=c: w_copy(z, c, left, w_left, True).start())

    def cols(zz, p):
        start = ((zz * n_y + p % n_y) * n_groups + p // n_y) * part
        return acts.at[:, pl.ds(pl.multiple_of(start, part), part)]

    def a_copy(zz, j):
        p = (me + j) % PLANE
        return remote(
            cols(zz, p), abuf.at[head * half_z + zz, me], a_send.at[j, zz], a_recv.at[j, zz], chip(p)
        )

    def a_arrived(zz, j):
        q = (me + PLANE - j) % PLANE
        return remote(
            cols(zz, me), abuf.at[head * half_z + zz, q], a_send.at[j, zz], a_recv.at[j, zz], chip(q)
        )

    def f_copy(zz, j):
        q = (me + PLANE - j) % PLANE
        slot = abuf.at[head * half_z + zz, q]
        src = cols(zz, me) if j == 0 else slot
        return remote(src, slot, f_send.at[j, zz], f_recv.at[j, zz], sibling)

    def f_arrived(zz, j):
        q = (me + PLANE - j) % PLANE
        slot = abuf.at[(1 - head) * half_z + zz, q]
        return remote(slot, slot, f_send.at[j, zz], f_recv.at[j, zz], sibling)

    def own_a(zz):
        return pltpu.make_async_copy(cols(zz, me), abuf.at[head * half_z + zz, me], loc_a.at[zz])

    def own_w(c):
        return pltpu.make_async_copy(w_own[c], wbuf.at[z, c], loc_w.at[c])

    @pl.loop(0, half_z)
    def _(zz):
        for j in range(1, PLANE):
            a_copy(zz, j).start()

    @pl.loop(0, half_z)
    def _(zz):
        own_a(zz).start()
        f_copy(zz, 0).start()

    for c in range(2):
        own_w(c).start()
    acc[...] = jnp.zeros_like(acc)

    def w_step(s, forward):
        for c in range(2):
            from_left = z - 1 - s
            from_right = z + 1 + s

            @pl.when(from_left >= 0)
            def _():
                w_copy(from_left, c, right, w_right, False).wait_recv()
                if forward:
                    pl.when(has_right)(lambda: w_copy(from_left, c, right, w_right, False).start())

            @pl.when(from_right <= n_z - 1)
            def _():
                w_copy(from_right, c, left, w_left, False).wait_recv()
                if forward:
                    pl.when(has_left)(lambda: w_copy(from_right, c, left, w_left, False).start())

    @pl.loop(0, n_z - 2)
    def _(s):
        w_step(s, True)

    @pl.loop(0, half_z)
    def _(zz):
        for j in range(1, PLANE):
            a_arrived(zz, j).wait_recv()
            f_copy(zz, j).start()

    for c in range(2):
        own_w(c).wait()

    @pl.loop(0, half_z)
    def _(zz):
        own_a(zz).wait()

    @pl.loop(0, half_z)
    def _(zz):
        for j in range(PLANE):
            f_arrived(zz, j).wait_recv()

    def multiply(block):
        @pl.loop(0, PLANE)
        def _(p):
            for c in range(2):
                acc[p, :, c * width : (c + 1) * width] += jnp.dot(
                    abuf[block, p], wbuf[block, c], preferred_element_type=jnp.float32
                )

    @pl.loop(0, n_z)
    def _(block):
        pl.when((block - z < n_z - 1) & (z - block < n_z - 1))(lambda: multiply(block))

    w_step(n_z - 2, False)
    pl.when(z == 0)(lambda: multiply(n_z - 1))
    pl.when(z == n_z - 1)(lambda: multiply(0))

    def r_copy(j):
        p = (me + j) % PLANE
        return remote(sbuf.at[j - 1], rbuf.at[j - 1], r_send.at[j], r_recv.at[j], chip(p))

    for j in (2, 1, 3):
        sbuf[j - 1] = acc[(me + j) % PLANE].astype(jnp.bfloat16)
        r_copy(j).start()
    total = acc[me]
    for j in (1, 3, 2):
        r_copy(j).wait_recv()
        total += rbuf[j - 1].astype(jnp.float32)
    gbuf[fsdp] = total.astype(jnp.bfloat16)

    def g_copy(zz, dev, send, recv):
        slot = gbuf.at[zz * n_y + y]
        return remote(slot, slot, send.at[zz], recv.at[zz], dev)

    cross = (group, z * n_y + (n_y - 1 - y), head)

    def g_start(zz, to_right, to_left):
        if to_right:
            pl.when(has_right)(lambda: g_copy(zz, right, g_right, g_recv).start())
        if to_left:
            pl.when(has_left)(lambda: g_copy(zz, left, g_left, g_recv).start())
        if n_y == 2:
            g_copy(zz, cross, g_cross, c_recv).start()

    g_start(z, True, True)

    @pl.loop(0, n_z - 1)
    def _(s):
        from_left = z - 1 - s
        from_right = z + 1 + s

        @pl.when(from_left >= 0)
        def _():
            g_copy(from_left, right, g_right, g_recv).wait_recv()
            g_start(from_left, True, False)

        @pl.when(from_right <= n_z - 1)
        def _():
            g_copy(from_right, left, g_left, g_recv).wait_recv()
            g_start(from_right, False, True)

    if n_y == 2:
        @pl.loop(0, n_z)
        def _(zz):
            slot = gbuf.at[zz * n_y + (1 - y)]
            remote(slot, slot, g_cross.at[zz], c_recv.at[zz], cross).wait_recv()

    done = pltpu.make_async_copy(gbuf, out, loc_out)
    done.start()

    for j in range(1, PLANE):
        r_copy(j).wait_send()

    @pl.loop(0, half_z)
    def _(zz):
        for j in range(1, PLANE):
            a_copy(zz, j).wait_send()
        for j in range(PLANE):
            f_copy(zz, j).wait_send()

    @pl.loop(0, n_z)
    def _(block):
        @pl.when((block <= z) & has_right)
        def _():
            for c in range(2):
                w_copy(block, c, right, w_right, False).wait_send()
            g_copy(block, right, g_right, g_recv).wait_send()

        @pl.when((block >= z) & has_left)
        def _():
            for c in range(2):
                w_copy(block, c, left, w_left, False).wait_send()
            g_copy(block, left, g_left, g_recv).wait_send()

        if n_y == 2:
            g_copy(block, cross, g_cross, c_recv).wait_send()

    done.wait()


def project(mesh_sizes, activations, w_key, w_value):
    n_groups, n_fsdp = mesh_sizes
    n_y = PLANE // n_groups
    n_z = n_fsdp // n_y
    rows = activations.shape[0]
    depth, width = w_key.shape
    part = depth // n_groups
    any_space = pl.BlockSpec(memory_space=pl.ANY)
    dma = pltpu.SemaphoreType.DMA
    half_z = n_z // 2
    return pl.pallas_call(
        functools.partial(rows_kernel, n_groups, n_z, n_y),
        out_shape=jax.ShapeDtypeStruct((n_fsdp, rows, 2 * width), jnp.bfloat16),
        in_specs=[any_space] * 3,
        out_specs=any_space,
        scratch_shapes=[
            pltpu.VMEM((n_z, PLANE, rows, part), jnp.bfloat16),
            pltpu.VMEM((n_z, 2, part, width), jnp.bfloat16),
            pltpu.VMEM((PLANE, rows, 2 * width), jnp.float32),
            pltpu.VMEM((PLANE - 1, rows, 2 * width), jnp.bfloat16),
            pltpu.VMEM((PLANE - 1, rows, 2 * width), jnp.bfloat16),
            pltpu.VMEM((n_fsdp, rows, 2 * width), jnp.bfloat16),
            dma((n_z, 2)),
            dma((n_z, 2)),
            dma((n_z, 2)),
            dma((PLANE, half_z)),
            dma((PLANE, half_z)),
            dma((PLANE, half_z)),
            dma((PLANE, half_z)),
            dma((PLANE,)),
            dma((PLANE,)),
            dma((n_z,)),
            dma((n_z,)),
            dma((n_z,)),
            dma((n_z,)),
            dma((n_z,)),
            dma((2,)),
            dma((half_z,)),
            dma,
        ],
        compiler_params=pltpu.CompilerParams(
            collective_id=0, has_side_effects=True, vmem_limit_bytes=48 * 2**20
        ),
    )(activations, w_key, w_value)


def token_docs(first_tok, count, doc_ends):
    positions = first_tok + jnp.arange(count, dtype=jnp.int32)
    pages = positions // PAGE
    found = jnp.sum((doc_ends[None, :] <= pages[:, None]).astype(jnp.int32), axis=1)
    return (jnp.where(positions >= 0, found, -1), positions)


def masked_scores(query_head, key_head, visible, score_scale):
    scores = (
        jnp.einsum("tqd,sd->qts", query_head, key_head, preferred_element_type=jnp.float32)
        * score_scale
    )
    return jnp.where(visible[None], scores, -1e30)


def per_device(mesh_sizes, activations, queries, w_key, w_value, request_pages, request_owner):
    tok_rows = activations.shape[0]
    width_kv = w_key.shape[1]
    kv_here = width_kv // HD
    per_group = QH // KVH
    my_index = lax.axis_index("fsdp")
    score_scale = HD ** (-0.5)
    gathered = project(mesh_sizes, activations, w_key, w_value)
    gathered = gathered.reshape(-1, 2 * width_kv)
    doc_ends = jnp.cumsum(request_pages)
    doc_begins = doc_ends - request_pages
    first_tok = my_index * tok_rows
    query_docs, query_pos = token_docs(first_tok, tok_rows, doc_ends)
    margin = SPAN * tok_rows
    padded = jnp.concatenate([jnp.zeros((margin, 2 * width_kv), jnp.bfloat16), gathered], axis=0)
    window = lax.dynamic_slice(padded, (first_tok, 0), (margin + tok_rows, 2 * width_kv))
    key_docs, key_pos = token_docs(first_tok - margin, margin + tok_rows, doc_ends)
    visible = (key_docs[None, :] == query_docs[:, None]) & (key_pos[None, :] <= query_pos[:, None])
    query_all = queries.reshape(tok_rows, kv_here, per_group, HD)
    head_outputs = []
    for kv_index in range(kv_here):
        query_head = query_all[:, kv_index]
        low = kv_index * HD
        key_head = window[:, low : low + HD]
        value_head = window[:, width_kv + low : width_kv + low + HD]
        scores = masked_scores(query_head, key_head, visible, score_scale)
        row_top = jnp.max(scores, axis=-1, keepdims=True)
        expo = jnp.where(visible[None], jnp.exp(scores - row_top), 0.0)
        row_total = jnp.sum(expo, axis=-1)
        weights = expo.astype(jnp.bfloat16)
        weighted = jnp.einsum(
            "qts,sd->tqd", weights, value_head, preferred_element_type=jnp.float32
        )
        head_outputs.append(weighted / jnp.transpose(row_total, (1, 0))[:, :, None])
    attended = (
        jnp.stack(head_outputs, axis=1)
        .reshape(tok_rows, kv_here * per_group * HD)
        .astype(jnp.bfloat16)
    )
    pages_here = tok_rows // PAGE
    cache_pages = SPAN * pages_here + 1
    owned = request_owner == my_index
    begin = jnp.sum(jnp.where(owned, doc_begins, 0))
    count = jnp.sum(jnp.where(owned, request_pages, 0))
    tail = jnp.zeros((cache_pages * PAGE, 2 * width_kv), jnp.bfloat16)
    pages = lax.dynamic_slice(
        jnp.concatenate([gathered, tail], axis=0),
        (begin * PAGE, 0),
        (cache_pages * PAGE, 2 * width_kv),
    ).reshape(cache_pages, PAGE, 2, width_kv)
    held = jnp.arange(cache_pages, dtype=jnp.int32) < count
    kv_cache = jnp.where(held[:, None, None, None], jnp.transpose(pages, (0, 2, 1, 3)), 0)
    kv_cache = kv_cache.astype(jnp.bfloat16)
    return (attended, kv_cache)


def solution(mesh):
    mesh_sizes = (mesh.shape["groups"], mesh.shape["fsdp"])
    return jax.shard_map(
        functools.partial(per_device, mesh_sizes),
        mesh=mesh,
        in_specs=(
            P(("groups", "fsdp"), "head"),
            P(("groups", "fsdp"), "head"),
            P("fsdp", "head"),
            P("fsdp", "head"),
            P("groups"),
            P("groups"),
        ),
        out_specs=(P(("groups", "fsdp"), "head"), P(("groups", "fsdp"), None, None, "head")),
        check_vma=False,
    )
```

time: 416 us -> 165 us (0.40)
  the two profiles are of different devices: /device:TPU:14 before, /device:TPU:0 now
where the time goes in v2:
time: 165 us; the launch traced here: 164 us
  Pallas kernels  111 us (67%)
  matrix products  32.1 us (19%)
  local copies, waits for them, and re-layouts  14.5 us (9%)
  other arithmetic  5.2 us (3%)
    pallas_call x1, Pallas kernels, project(): pl.pallas_call(functools.partial(rows_kernel, n_groups, n_z, n_y), out_sh...  111 us
    sub x2, matrix products, per_device(): expo = jnp.where(visible[None], jnp.exp(scores - row_top), 0.0)  22.3 us
    unnamed x11, local copies, waits for them, and re-layouts  10.5 us
    dot_general x2, matrix products, per_device(): jnp.einsum('qts,sd->tqd', weights, value_head, preferred_element_type=jnp...  9.82 us

profile of v2, /device:TPU:0, one launch (start us, length us, event | category | flops | bytes accessed | tf_op | source)
XLA Modules:
  0.0 164.4 jit_solution(17360595701247932142)
XLA Ops:
  0.6 0.0 copy-start
  0.7 0.9 reduce-window.8
  1.6 0.1 convert_reduce_fusion.1
  1.7 0.1 convert_reduce_fusion
  1.8 0.3 compare_and_fusion
  2.1 4.1 %copy.22 = bf16[256,4096]{0,1:T(8,128)(2,1)} copy(bf16[256,4096]{1,0:T(8,128)(2,1)} %param.7) | data formatting | bytes 4194304 | tf_op args[1]
  6.2 0.0 copy-done
  6.2 1.2 copy-done.1
  7.4 111.2 %shard_map.77 = bf16[8,256,512]{2,1,0:T(8,128)(2,1)S(1)} custom-call(bf16[256,8192]{1,0:T(8,128)(2,1)} %acts.1, bf16[2048,256]{1,0:T(8,128)(2,1)S(1)} %copy-done, bf16[2048,256]{1,0:T(8,128)(2,1)S(1)} %copy-done.1), custom_call_target="tpu_custom_call" | custom-call | tf_op jit(solution)/shard_map/pallas_call | solution.py:265
  118.6 11.1 %fusion.56 = (f32[16,256]{1,0:T(8,128)S(1)}, bf16[16,256,1024]{1,2,0:T(8,128)(2,1)}) fusion(pred[256,1024]{0,1:T(8,128)(4,1)S(1)} %compare_and_fusion, bf16[256,2,16,128]{0,3,2,1:T(8,128)(2,1)} %bitcast.110, s32[]{:T(128)S(6)} %select_n.67, s32[]{:T(128)S(6)} %add.62, bf16[2048,512]{1,0:T(8,128)(2,1)S(1)} %bitcast.104), kind=kOutput, calls=%fused_computation.75 | convolution fusion | flops 1098908672 | bytes 12075016 | tf_op jit(solution)/shard_map/sub | solution.py:343
  129.8 4.9 %fusion.27 = bf16[256,1,16,128]{0,3,2,1:T(8,128)(2,1)S(1)} fusion(bf16[16,256,1024]{1,2,0:T(8,128)(2,1)} %get-tuple-element.11, f32[256,16]{0,1:T(8,128)S(1)} %bitcast.116, s32[]{:T(128)S(6)} %select_n.67, s32[]{:T(128)S(6)} %add.61, bf16[2048,512]{1,0:T(8,128)(2,1)S(1)} %bitcast.105), kind=kOutput, calls=%fused_computation.32 | convolution fusion | flops 1074790400 | bytes 11550728 | tf_op jit(solution)/shard_map/qts,sd->tqd/dot_general | solution.py:346
  134.7 11.2 %fusion.61 = (f32[16,256]{1,0:T(8,128)S(1)}, bf16[16,256,1024]{1,2,0:T(8,128)(2,1)}) fusion(pred[256,1024]{0,1:T(8,128)(4,1)S(1)} %compare_and_fusion, bf16[256,2,16,128]{0,3,2,1:T(8,128)(2,1)} %bitcast.111, s32[]{:T(128)S(6)} %select_n.67, bf16[2048,512]{1,0:T(8,128)(2,1)S(1)} %bitcast.106), kind=kOutput, calls=%fused_computation.76 | convolution fusion | flops 1098908672 | bytes 12075012 | tf_op jit(solution)/shard_map/sub | solution.py:343
  145.8 4.9 %fusion.24 = bf16[256,1,16,128]{0,3,2,1:T(8,128)(2,1)S(1)} fusion(bf16[16,256,1024]{1,2,0:T(8,128)(2,1)} %get-tuple-element.13, f32[256,16]{0,1:T(8,128)S(1)} %bitcast.115, s32[]{:T(128)S(6)} %select_n.67, s32[]{:T(128)S(6)} %add.60, bf16[2048,512]{1,0:T(8,128)(2,1)S(1)} %bitcast.107), kind=kOutput, calls=%fused_computation.31 | convolution fusion | flops 1074790400 | bytes 11550728 | tf_op jit(solution)/shard_map/qts,sd->tqd/dot_general | solution.py:346
  150.8 0.0 copy-start.2
  150.8 0.0 copy-start.3
  150.8 1.5 pad_maximum_fusion
  152.3 4.1 %copy.29 = bf16[256,4096]{1,0:T(8,128)(2,1)} copy(bf16[256,4096]{0,1:T(8,128)(2,1)} %bitcast.109) | data formatting | bytes 4194304
  156.4 0.0 copy-done.2
  156.4 0.7 fusion.48
  157.8 1.6 pad_dynamic-slice_fusion.4
  159.4 2.4 %reshape.161 = bf16[7,128,2,256]{3,2,1,0:T(2,128)(2,1)S(1)} reshape(bf16[896,512]{1,0:T(8,128)(2,1)} %pad_dynamic-slice_fusion.4) | data formatting | bytes 1835008 | tf_op jit(solution)/shard_map/reshape | solution.py:365
  161.8 0.7 iota_compare_fusion
  162.5 0.8 fusion.32
  163.3 1.1 copy.30
  (6 shorter events, 0.0 us)
Async XLA Ops:
  0.6 5.6 %copy-start = (bf16[2048,256]{1,0:T(8,128)(2,1)S(1)}, bf16[2048,256]{1,0:T(8,128)(2,1)}, u32[]{:S(2)}) copy-start(bf16[2048,256]{1,0:T(8,128)(2,1)} %w_key.1) | copy-start | bytes 3145732
  6.2 1.2 copy-start.1
  150.8 5.6 %copy-start.2 = (s32[8]{0:T(128)S(1)}, s32[8]{0:T(128)}, u32[]{:S(2)}) copy-start(s32[8]{0:T(128)} %param.10) | copy-start | bytes 100
  150.8 5.6 %copy-start.3 = (s32[8]{0:T(128)S(1)}, s32[8]{0:T(128)}, u32[]{:S(2)}) copy-start(s32[8]{0:T(128)} %param.11) | copy-start | bytes 100

commit v3 on v2

--- a/solution.py
+++ b/solution.py
@@ -6,8 +6,6 @@
 from jax.experimental.pallas import tpu as pltpu
 from jax.sharding import PartitionSpec as P
 
-QH = 64
-KVH = 4
 HD = 128
 PAGE = 128
 SPAN = 3
@@ -298,75 +296,103 @@
     )(activations, w_key, w_value)
 
 
-def token_docs(first_tok, count, doc_ends):
-    positions = first_tok + jnp.arange(count, dtype=jnp.int32)
-    pages = positions // PAGE
-    found = jnp.sum((doc_ends[None, :] <= pages[:, None]).astype(jnp.int32), axis=1)
-    return (jnp.where(positions >= 0, found, -1), positions)
-
-
-def masked_scores(query_head, key_head, visible, score_scale):
-    scores = (
-        jnp.einsum("tqd,sd->qts", query_head, key_head, preferred_element_type=jnp.float32)
-        * score_scale
-    )
-    return jnp.where(visible[None], scores, -1e30)
+def attend_kernel(per_group, info, queries, blocks, attended, cache):
+    kv_index, page = pl.program_id(0), pl.program_id(1)
+    block_rows = blocks.shape[1]
+    width = blocks.shape[2] // 2
+    kv_here = width // HD
+    my_block = info[0]
+    begin = info[1 + page]
+    per_block = block_rows // PAGE
+    first_block = begin // per_block
+    q_pos = (my_block * per_block + page) * PAGE + lax.broadcasted_iota(jnp.int32, (PAGE, 1), 0)
+    factor = HD ** -0.5 * 1.4426950408889634
+
+    def run(kv, count):
+        k_pos = first_block * block_rows + lax.broadcasted_iota(
+            jnp.int32, (1, count * block_rows), 1
+        )
+        bias = jnp.where((k_pos >= begin * PAGE) & (k_pos <= q_pos), 0.0, -1e30)
+        low = kv * HD
+        keys = [blocks[first_block + i, :, low : low + HD] for i in range(count)]
+        values = [blocks[first_block + i, :, width + low : width + low + HD] for i in range(count)]
+        keys = jnp.concatenate(keys, axis=0)
+        values = jnp.concatenate(values, axis=0)
+        for h in range(per_group):
+            at = slice(h * HD, (h + 1) * HD)
+            scores = lax.dot_general(
+                queries[:, at], keys, (((1,), (1,)), ((), ())), preferred_element_type=jnp.float32
+            )
+            scores = scores + bias
+            top = jnp.max(scores, axis=1, keepdims=True)
+            expo = jnp.exp2((scores - top) * factor)
+            total = jnp.sum(expo, axis=1, keepdims=True)
+            mixed = jnp.dot(expo.astype(jnp.bfloat16), values, preferred_element_type=jnp.float32)
+            attended[:, at] = (mixed / total).astype(jnp.bfloat16)
+
+    for kv in range(kv_here):
+        for count in range(1, SPAN + 2):
+            pl.when((kv_index == kv) & (my_block - first_block == count - 1))(
+                functools.partial(run, kv, count)
+            )
+
+    @pl.when((kv_index == 0) & (page == 0))
+    def _():
+        base, pages = info[1 + per_block], info[2 + per_block]
+        last = blocks.shape[0] * per_block - 1
+        for slot in range(cache.shape[0]):
+            source = jnp.minimum(base + slot, last)
+            rows = pl.ds(pl.multiple_of((source % per_block) * PAGE, PAGE), PAGE)
+            data = blocks[source // per_block, rows, :]
+            data = jnp.where(slot < pages, data, jnp.zeros_like(data))
+            cache[slot, 0] = data[:, :width]
+            cache[slot, 1] = data[:, width:]
+
+
+def attend(info, queries, gathered, kv_here, cache_pages):
+    rows, q_width = queries.shape
+    n_blocks, block_rows, width = gathered.shape
+    group_width = q_width // kv_here
+    return pl.pallas_call(
+        functools.partial(attend_kernel, group_width // HD),
+        out_shape=(
+            jax.ShapeDtypeStruct((rows, q_width), jnp.bfloat16),
+            jax.ShapeDtypeStruct((cache_pages, 2, PAGE, width // 2), jnp.bfloat16),
+        ),
+        grid_spec=pltpu.PrefetchScalarGridSpec(
+            num_scalar_prefetch=1,
+            grid=(kv_here, rows // PAGE),
+            in_specs=[
+                pl.BlockSpec((PAGE, group_width), lambda kv, page, info: (page, kv)),
+                pl.BlockSpec((n_blocks, block_rows, width), lambda kv, page, info: (0, 0, 0)),
+            ],
+            out_specs=[
+                pl.BlockSpec((PAGE, group_width), lambda kv, page, info: (page, kv)),
+                pl.BlockSpec(
+                    (cache_pages, 2, PAGE, width // 2), lambda kv, page, info: (0, 0, 0, 0)
+                ),
+            ],
+        ),
+        compiler_params=pltpu.CompilerParams(
+            dimension_semantics=("arbitrary", "arbitrary"), vmem_limit_bytes=48 * 2**20
+        ),
+    )(info, queries, gathered)
 
 
 def per_device(mesh_sizes, activations, queries, w_key, w_value, request_pages, request_owner):
-    tok_rows = activations.shape[0]
-    width_kv = w_key.shape[1]
-    kv_here = width_kv // HD
-    per_group = QH // KVH
     my_index = lax.axis_index("fsdp")
-    score_scale = HD ** (-0.5)
     gathered = project(mesh_sizes, activations, w_key, w_value)
-    gathered = gathered.reshape(-1, 2 * width_kv)
+    pages_here = activations.shape[0] // PAGE
     doc_ends = jnp.cumsum(request_pages)
     doc_begins = doc_ends - request_pages
-    first_tok = my_index * tok_rows
-    query_docs, query_pos = token_docs(first_tok, tok_rows, doc_ends)
-    margin = SPAN * tok_rows
-    padded = jnp.concatenate([jnp.zeros((margin, 2 * width_kv), jnp.bfloat16), gathered], axis=0)
-    window = lax.dynamic_slice(padded, (first_tok, 0), (margin + tok_rows, 2 * width_kv))
-    key_docs, key_pos = token_docs(first_tok - margin, margin + tok_rows, doc_ends)
-    visible = (key_docs[None, :] == query_docs[:, None]) & (key_pos[None, :] <= query_pos[:, None])
-    query_all = queries.reshape(tok_rows, kv_here, per_group, HD)
-    head_outputs = []
-    for kv_index in range(kv_here):
-        query_head = query_all[:, kv_index]
-        low = kv_index * HD
-        key_head = window[:, low : low + HD]
-        value_head = window[:, width_kv + low : width_kv + low + HD]
-        scores = masked_scores(query_head, key_head, visible, score_scale)
-        row_top = jnp.max(scores, axis=-1, keepdims=True)
-        expo = jnp.where(visible[None], jnp.exp(scores - row_top), 0.0)
-        row_total = jnp.sum(expo, axis=-1)
-        weights = expo.astype(jnp.bfloat16)
-        weighted = jnp.einsum(
-            "qts,sd->tqd", weights, value_head, preferred_element_type=jnp.float32
-        )
-        head_outputs.append(weighted / jnp.transpose(row_total, (1, 0))[:, :, None])
-    attended = (
-        jnp.stack(head_outputs, axis=1)
-        .reshape(tok_rows, kv_here * per_group * HD)
-        .astype(jnp.bfloat16)
-    )
-    pages_here = tok_rows // PAGE
-    cache_pages = SPAN * pages_here + 1
+    own_pages = my_index * pages_here + jnp.arange(pages_here, dtype=jnp.int32)
+    inside = (doc_begins[None, :] <= own_pages[:, None]) & (own_pages[:, None] < doc_ends[None, :])
+    begins = jnp.sum(jnp.where(inside, doc_begins[None, :], 0), axis=1)
     owned = request_owner == my_index
-    begin = jnp.sum(jnp.where(owned, doc_begins, 0))
+    base = jnp.sum(jnp.where(owned, doc_begins, 0))
     count = jnp.sum(jnp.where(owned, request_pages, 0))
-    tail = jnp.zeros((cache_pages * PAGE, 2 * width_kv), jnp.bfloat16)
-    pages = lax.dynamic_slice(
-        jnp.concatenate([gathered, tail], axis=0),
-        (begin * PAGE, 0),
-        (cache_pages * PAGE, 2 * width_kv),
-    ).reshape(cache_pages, PAGE, 2, width_kv)
-    held = jnp.arange(cache_pages, dtype=jnp.int32) < count
-    kv_cache = jnp.where(held[:, None, None, None], jnp.transpose(pages, (0, 2, 1, 3)), 0)
-    kv_cache = kv_cache.astype(jnp.bfloat16)
-    return (attended, kv_cache)
+    info = jnp.concatenate([my_index[None], begins, base[None], count[None]]).astype(jnp.int32)
+    return attend(info, queries, gathered, w_key.shape[1] // HD, SPAN * pages_here + 1)
 
 
 def solution(mesh):

time: 165 us -> 140 us (0.85)
  the two profiles are of different devices: /device:TPU:0 before, /device:TPU:14 now
where the time goes in v3:
time: 140 us
  Pallas kernels  133 us (95%)
  other arithmetic  3.82 us (3%)
  local copies, waits for them, and re-layouts  2.45 us (2%)
    pallas_call x1, Pallas kernels, project(): pl.pallas_call(functools.partial(rows_kernel, n_groups, n_z, n_y), out_sh...  108 us
    pallas_call x1, Pallas kernels, attend(): pl.pallas_call(functools.partial(attend_kernel, group_width // HD), out_s...  25.5 us

profile of v3, /device:TPU:14, one launch (start us, length us, event | category | flops | bytes accessed | tf_op | source)
XLA Modules:
  0.0 140.0 jit_solution(3072863141304885248)
XLA Ops:
  0.6 0.8 reduce-window.8
  1.5 1.4 fusion.1
  2.9 0.2 fusion
  3.1 1.4 %pad_add_fusion.info = s32[5]{0:T(128)S(1)} fusion(s32[1]{0:T(128)} %bitcast.4, s32[1]{0:T(128)} %bitcast.3, s32[2]{0:T(128)S(1)} %fusion, s32[1]{0:T(128)} %bitcast), kind=kLoop, calls=%fused_computation.6 | loop fusion | flops 15 | bytes 40 | tf_op jit(solution)/shard_map/concatenate | solution.py:394
  4.5 0.0 copy-start.1
  4.5 1.2 copy-done.1
  5.7 0.0 copy-start.2
  5.7 1.2 copy-done.2
  6.9 0.0 copy-start
  6.9 107.6 %shard_map.77.blocks = bf16[8,256,512]{2,1,0:T(8,128)(2,1)S(1)} custom-call(bf16[256,8192]{1,0:T(8,128)(2,1)} %acts.1, bf16[2048,256]{1,0:T(8,128)(2,1)S(1)} %copy-done.1, bf16[2048,256]{1,0:T(8,128)(2,1)S(1)} %copy-done.2), custom_call_target="tpu_custom_call" | custom-call | tf_op jit(solution)/shard_map/pallas_call | solution.py:263
  114.5 0.0 copy-done
  114.5 25.5 %shard_map.78 = (bf16[256,4096]{1,0:T(8,128)(2,1)}, bf16[7,2,128,256]{3,2,1,0:T(8,128)(2,1)}) custom-call(s32[5]{0:T(128)S(1)} %pad_add_fusion.info, bf16[256,4096]{1,0:T(8,128)(2,1)S(1)} %copy-done, bf16[8,256,512]{2,1,0:T(8,128)(2,1)S(1)} %shard_map.77.blocks), custom_call_target="tpu_custom_call" | custom-call | tf_op jit(solution)/shard_map/pallas_call | solution.py:356
  (1 shorter events, 0.0 us)
Async XLA Ops:
  4.5 1.2 copy-start.1
  5.7 1.2 copy-start.2
  6.9 107.6 %copy-start = (bf16[256,4096]{1,0:T(8,128)(2,1)S(1)}, bf16[256,4096]{1,0:T(8,128)(2,1)}, u32[]{:S(2)}) copy-start(bf16[256,4096]{1,0:T(8,128)(2,1)} %queries.1) | copy-start | bytes 6291460
